TPU v7x, 128 devices: a whole 4x4x4 slice. The times are simulated.
128 devices in a mesh: grp: 8 (over z, core), dev: 16 (over x, y).
Axes of the slice: x: 4, y: 4, z: 4, core: 2. Of those that a mesh axis runs over, the one named last changes fastest.
Arguments:
- velocity_old: float32 [512, 3, 32, 1024], P(('grp', 'dev')), may hold values from -6 to 6
- viscosity_old: float32 [512, 32, 1024], P(('grp', 'dev')), may hold values from 0.25 to 4
- source: int32 [512], replicated, may hold values from 0 to 511, as said below
Outputs:
- velocity_new: float32 [512, 3, 32, 1024], P(('grp', 'dev'))
Inputs may be any that keep to these rules, and one draw needn't show every extreme that they name: `source`: A permutation; the old block of new block b lies in the same agglomeration group and has the same place among its device's 4 blocks; the 4 blocks of a new device come from 4 different old devices of its group, and each old device sends 1 block to each of 4 different new devices.
All inputs are finite; a program needn't handle non-finite values.
Results may differ from a plain program's by a relative error of at most 0.0001.
Values sent between devices are 32-bit elements; how exact they have to be, the bound alone decides.
A program may use at most 256 MiB of HBM per device.

v0:
```python
import math
import jax
import jax.numpy as jnp
from jax import lax
from jax.sharding import PartitionSpec as P

SWEEPS = 2
BOTTOM = 8
RELAX_WEIGHT = 0.8
DIFFUSION_NUMBER = 1000.0


def padded_2(cells, sides, width):
    for axis, dim in sides:
        count = lax.axis_size(axis)
        ends = count - 1
        head = lax.slice_in_dim(cells, 0, width, axis=dim)
        tail = lax.slice_in_dim(cells, cells.shape[dim] - width, cells.shape[dim], axis=dim)
        cells = jnp.concatenate(
            [
                lax.ppermute(tail, axis, [(i, (i + 1) % count) for i in range(ends)]),
                cells,
                lax.ppermute(head, axis, [((i + 1) % count, i) for i in range(ends)]),
            ],
            axis=dim,
        )
    return cells


def blocks_to_grid(blocks):
    num_blocks, channels, edge_len = (blocks.shape[0], blocks.shape[1], blocks.shape[2])
    columns = num_blocks // 4
    parted = blocks.reshape(columns, 2, 2, channels, edge_len, edge_len, edge_len)
    parted = parted.transpose(3, 0, 6, 1, 4, 2, 5)
    return parted.reshape(channels, columns * edge_len, 4 * edge_len * edge_len)


def grid_to_blocks(grid):
    channels, length, plane = grid.shape
    edge_len = math.isqrt(plane) // 2
    columns = length // edge_len
    parted = grid.reshape(channels, columns, edge_len, 2, edge_len, 2, edge_len)
    parted = parted.transpose(1, 3, 5, 0, 4, 6, 2)
    return parted.reshape(columns * 4, channels, edge_len, edge_len * edge_len)


def flat_neighbors(array):
    plane = array.shape[2]
    width_y = math.isqrt(plane)
    middle = array[:, 1:-1]
    padded = jnp.pad(middle, ((0, 0), (0, 0), (width_y, width_y)))
    column = jnp.arange(plane) % width_y
    lower_y = jnp.where(column == 0, 0.0, padded[:, :, width_y - 1 : width_y - 1 + plane])
    upper_y = jnp.where(column == width_y - 1, 0.0, padded[:, :, width_y + 1 : width_y + 1 + plane])
    return (
        middle,
        (
            array[:, :-2],
            array[:, 2:],
            padded[:, :, 0:plane],
            padded[:, :, 2 * width_y : 2 * width_y + plane],
            lower_y,
            upper_y,
        ),
    )


def coefficients(viscous, level_coef, pad_along):
    middle, beside_all = flat_neighbors(pad_along(viscous))
    face_coef = tuple((0.5 * (middle + neighbor) for neighbor in beside_all))
    summed = face_coef[0] + face_coef[1] + face_coef[2] + face_coef[3] + face_coef[4] + face_coef[5]
    diagonal = 1.0 + level_coef * summed
    return (face_coef, diagonal)


def operate(solution, face_coef, diagonal, level_coef, pad_along):
    middle, beside_all = flat_neighbors(pad_along(solution))
    summed = face_coef[0] * beside_all[0]
    for index_no in range(1, 6):
        summed = summed + face_coef[index_no] * beside_all[index_no]
    return diagonal * solution - level_coef * summed


def smooth(solution, right_side, face_coef, diagonal, level_coef, pad_along, repeats):
    for sweep_no in range(repeats):
        solution = (
            solution
            + RELAX_WEIGHT
            * (right_side - operate(solution, face_coef, diagonal, level_coef, pad_along))
            / diagonal
        )
    return solution


def coarsen(grid):
    channels, length, plane = grid.shape
    width_y = math.isqrt(plane)
    shaped = grid.reshape(channels, length // 2, 2, width_y // 2, 2, width_y // 2, 2)
    return shaped.mean(axis=(2, 4, 6)).reshape(channels, length // 2, plane // 4)


def refine(grid):
    channels, length, plane = grid.shape
    width_y = math.isqrt(plane)
    shaped = grid.reshape(channels, length, 1, width_y, 1, width_y, 1)
    shaped = jnp.broadcast_to(shaped, (channels, length, 2, width_y, 2, width_y, 2))
    return shaped.reshape(channels, 2 * length, 4 * plane)


def cell_pad(array):
    return padded_2(array, ((("grp", "dev"), 1),), 1)


def group_pad(array):
    return padded_2(array, (("grp", 1),), 1)


def group_bottom(level_rhs, viscous):
    stacked = jnp.concatenate([level_rhs, viscous], axis=0)
    gathered = lax.all_gather(stacked, "dev", axis=1, tiled=True)
    group_rhs = gathered[:3]
    group_visc = gathered[3:]
    level_coef = DIFFUSION_NUMBER / 64.0
    face_coef, diagonal = coefficients(group_visc, level_coef, group_pad)
    solved = smooth(
        jnp.zeros_like(group_rhs), group_rhs, face_coef, diagonal, level_coef, group_pad, BOTTOM
    )
    own_width = level_rhs.shape[1]
    return lax.dynamic_slice_in_dim(solved, lax.axis_index("dev") * own_width, own_width, 1)


def vcycle_solve(right_side, viscous):
    stored = []
    solution = right_side
    level_rhs = right_side
    for level_no in range(3):
        level_coef = DIFFUSION_NUMBER / 4.0**level_no
        face_coef, diagonal = coefficients(viscous, level_coef, cell_pad)
        solution = smooth(solution, level_rhs, face_coef, diagonal, level_coef, cell_pad, SWEEPS)
        residue = level_rhs - operate(solution, face_coef, diagonal, level_coef, cell_pad)
        stored.append((solution, level_rhs, face_coef, diagonal, level_coef))
        level_rhs = coarsen(residue)
        viscous = coarsen(viscous)
        solution = jnp.zeros_like(level_rhs)
    solution = group_bottom(level_rhs, viscous)
    for level_no in (2, 1, 0):
        before, level_rhs, face_coef, diagonal, level_coef = stored[level_no]
        solution = smooth(
            before + refine(solution), level_rhs, face_coef, diagonal, level_coef, cell_pad, SWEEPS
        )
    return solution


def local(velocity_old, viscosity_old, source):
    group_index = lax.axis_index("grp")
    member_index = lax.axis_index("dev")
    member_count = lax.axis_size("dev")
    blk_per = velocity_old.shape[0]
    group_base = group_index * member_count * blk_per
    src_table = (
        lax.dynamic_slice_in_dim(source, group_base, member_count * blk_per).reshape(
            member_count, blk_per
        )
        - group_base
    )
    from_dev = src_table // blk_per
    from_slot = src_table % blk_per
    mine_dev = lax.dynamic_index_in_dim(from_dev, member_index, 0, keepdims=False)
    mine_slot = lax.dynamic_index_in_dim(from_slot, member_index, 0, keepdims=False)
    wanted = mine_dev * blk_per + mine_slot
    pieces = (
        lax.all_gather(velocity_old, "dev", axis=0, tiled=True),
        lax.all_gather(viscosity_old, "dev", axis=0, tiled=True),
    )
    piece_rows = pieces[0].shape[0]
    inside = (wanted >= 0) & (wanted < piece_rows)
    clipped = jnp.clip(wanted, 0, piece_rows - 1)
    new_vel = jnp.where(
        inside[:, None, None, None],
        jnp.take(pieces[0], clipped, axis=0),
        jnp.zeros_like(velocity_old),
    )
    new_visc = jnp.where(
        inside[:, None, None], jnp.take(pieces[1], clipped, axis=0), jnp.zeros_like(viscosity_old)
    )
    right_side = blocks_to_grid(new_vel)
    viscous = blocks_to_grid(new_visc[:, None])
    solution = vcycle_solve(right_side, viscous)
    return grid_to_blocks(solution)


def solution(mesh):
    return jax.shard_map(
        local,
        mesh=mesh,
        in_specs=(P(("grp", "dev"), None, None, None), P(("grp", "dev"), None, None), P()),
        out_specs=P(("grp", "dev"), None, None, None),
        check_vma=False,
    )
```

profile of v0, /device:TPU:31, one launch (start us, length us, event | category | flops | bytes accessed | tf_op | source)
XLA Modules:
  0.0 1013.4 jit_solution(10775965139218544529)
XLA Ops:
  11.0 7.4 collective-permute-start.18
  22.6 57.7 %all-gather.5.cloned.1.call-done = f32[64,32,1024]{2,1,0:T(8,128)} async-done(((f32[4,32,1024]{2,1,0:T(8,128)}), f32[64,32,1024]{2,1,0:T(8,128)}) %all-gather.5.cloned.1.call-update) | async-done | bytes 8388624 | tf_op jit(solution)/shard_map/all_gather | solution.py:173
  80.3 4.0 gather_fusion.1
  86.7 22.0 %reshape_reshape.2 = f32[16,2,32,2,32,2]{1,0,5,4,3,2:T(8,128)} reshape(f32[1,1,32,2,32,2,32]{2,6,5,4,3,1,0:T(8,128)} %fusion.454) | data formatting | bytes 1048576 | tf_op jit(solution)/shard_map/reshape;reshape | solution.py:98
  108.7 12.5 %reduce_sum.55 = f32[16,32,32]{0,2,1:T(8,128)S(1)} reduce(f32[16,2,32,2,32,2]{1,0,5,4,3,2:T(8,128)} %reshape_reshape.2, f32[]{:T(128)} %constant.250.clone.1), dimensions={1,3,5}, to_apply=%region_1.2 | reduce | flops 114688 | bytes 589828 | tf_op jit(solution)/shard_map/reduce_sum | solution.py:99
  121.7 3.6 div.201
  129.3 5.6 collective-permute-start
  140.5 96.1 %all-gather.3.cloned.1.call-done = f32[64,3,32,1024]{3,2,1,0:T(8,128)} async-done(((f32[4,3,32,1024]{3,2,1,0:T(8,128)}), f32[64,3,32,1024]{3,2,1,0:T(8,128)}) %all-gather.3.cloned.1.call-update) | async-done | bytes 25165840 | tf_op jit(solution)/shard_map/all_gather | solution.py:172
  236.7 8.8 gather_fusion
  245.5 4.1 gather.13
  249.6 10.0 copy.71
  259.5 11.8 %select_bitcast_fusion = f32[3,1,32,2,32,2,32]{6,5,4,3,2,0,1:T(2,128)} fusion(f32[1,2,2,3,32,32,32]{5,2,4,1,6,3,0:T(2,128)} %copy.71, pred[2,2]{1,0:T(4,128)(4,1)S(1)} %compare_and_fusion, pred[2,2]{1,0:T(4,128)(4,1)S(1)} %and.182), kind=kLoop, calls=%fused_computation.2 | loop fusion | flops 786432 | bytes 3145736 | tf_op jit(solution)/shard_map/transpose | solution.py:34
  271.3 9.5 reshape.248
  280.9 5.5 collective-permute-start.2
  288.4 5.2 add_bitcast_fusion
  293.6 7.9 collective-permute-start.8
  305.5 7.9 collective-permute-start.4
  316.1 6.9 collective-permute-done.5
  331.2 6.4 collective-permute-start.10
  342.9 154.0 %reshape.250 = f32[3,16,2,32,2,32,2]{6,5,4,3,2,1,0:T(8,128)} reshape(f32[3,32,4096]{2,1,0:T(8,128)} %fusion.35) | data formatting | bytes 3145728 | tf_op jit(solution)/shard_map/reshape | solution.py:98
  496.9 31.6 %reduce_sum.54 = f32[3,16,32,32]{3,2,1,0:T(8,128)} reduce(f32[3,16,2,32,2,32,2]{6,5,4,3,2,1,0:T(8,128)} %reshape.250, f32[]{:T(128)} %constant.250.clone.1), dimensions={2,4,6}, to_apply=%region_0.1 | reduce | flops 344064 | bytes 1769476 | tf_op jit(solution)/shard_map/reduce_sum | solution.py:99
  532.2 3.5 collective-permute-start.17
  537.1 6.4 collective-permute-start.12
  546.8 5.9 collective-permute-done.13
  561.0 4.2 collective-permute-done.15
  566.8 14.7 %reshape.251 = f32[3,8,2,16,2,16,2]{6,5,4,3,2,1,0:T(8,128)} reshape(f32[3,16,1024]{2,1,0:T(8,128)} %fusion.106) | data formatting | bytes 393216 | tf_op jit(solution)/shard_map/reshape | solution.py:98
  581.6 6.3 reduce_sum.56
  599.2 3.6 collective-permute-start.26
  605.2 5.5 collective-permute-start.22
  613.1 6.7 collective-permute-done.23
  624.4 15.4 %all_gather.11 = f32[4,64,64]{2,0,1:T(4,128)S(1)} all-gather(f32[4,4,64]{2,0,1:T(4,128)S(1)} %copy.76), channel_id=1, replica_groups=mesh['grp'=8,'dev'=16] {'dev'}, dimensions={1}, use_global_device_ids=true | all-gather | bytes 69632 | tf_op jit(solution)/shard_map/all_gather | solution.py:120
  639.8 7.6 collective-permute-start.24
  711.9 4.1 collective-permute-start.42
  717.9 7.2 collective-permute-done.43
  730.6 5.8 collective-permute-done.45
  737.3 5.8 broadcast_in_dim.360
  743.1 10.4 %reshape.254 = f32[3,16,1024]{2,1,0:T(8,128)} reshape(f32[3,8,2,16,2,16,2]{6,5,4,3,2,1,0:T(8,128)} %broadcast_in_dim.360) | data formatting | bytes 393216 | tf_op jit(solution)/shard_map/reshape | solution.py:107
  759.9 5.9 collective-permute-done.47
  769.0 3.5 collective-permute-start.49
  772.5 5.7 collective-permute-done.49
  781.3 32.2 %broadcast_in_dim.362 = f32[3,16,2,32,2,32,2]{6,5,4,3,2,1,0:T(8,128)} broadcast(f32[3,16,32,32]{3,2,1,0:T(8,128)} %broadcast_in_dim.361), dimensions={0,1,3,5} | broadcast | bytes 1769472 | tf_op jit(solution)/shard_map/broadcast_in_dim | solution.py:106
  813.5 138.7 %reshape.255 = f32[3,32,4096]{2,1,0:T(8,128)} reshape(f32[3,16,2,32,2,32,2]{6,5,4,3,2,1,0:T(8,128)} %broadcast_in_dim.362) | data formatting | bytes 3145728 | tf_op jit(solution)/shard_map/reshape | solution.py:107
  959.8 6.3 collective-permute-done.51
  970.2 3.6 collective-permute-start.53
  973.8 6.0 collective-permute-done.53
  982.7 7.7 reshape.256
  990.4 10.1 copy.78
  1000.5 5.9 reshape.257
  (327 shorter events, 180.9 us)
Async XLA Ops:
  6.5 73.8 %all-gather.5.cloned.1.call-start = ((), (), s32[]{:S(2)}) async-start(), calls=%async_computation.1 | async-start | bytes 8912896 | tf_op jit(solution)/shard_map/all_gather | solution.py:173
  7.3 229.4 %all-gather.3.cloned.1.call-start = ((), (), s32[]{:S(2)}) async-start(), calls=%async_computation | async-start | bytes 26738688 | tf_op jit(solution)/shard_map/all_gather | solution.py:172
  8.6 581.9 %collective-permute-start.19 = (f32[3,1,256]{2,1,0:T(1,128)}, f32[3,1,256]{2,1,0:T(1,128)}, u32[]{:S(2)}, u32[]{:S(2)}) collective-permute-start(f32[3,1,256]{2,1,0:T(1,128)} %broadcast.449), channel_id=1, source_target_pairs={{1,0},{2,1},{3,2},{4,3},{5,4},{6,5},{7,6},{8,7},{9,8},{10,9},{11,1... | collective-permute-start | bytes 9224 | tf_op jit(solution)/shard_map/ppermute | solution.py:23
  11.0 579.6 %collective-permute-start.18 = (f32[3,1,256]{2,1,0:T(1,128)}, f32[3,1,256]{2,1,0:T(1,128)}, u32[]{:S(2)}, u32[]{:S(2)}) collective-permute-start(f32[3,1,256]{2,1,0:T(1,128)} %broadcast.449), channel_id=1, source_target_pairs={{0,1},{1,2},{2,3},{3,4},{4,5},{5,6},{6,7},{7,8},{8,9},{9,10},{10,1... | collective-permute-start | bytes 9224 | tf_op jit(solution)/shard_map/ppermute | solution.py:21
  19.0 513.2 %collective-permute-start.11 = (f32[3,1,1024]{2,1,0:T(1,128)}, f32[3,1,1024]{2,1,0:T(1,128)}, u32[]{:S(2)}, u32[]{:S(2)}) collective-permute-start(f32[3,1,1024]{2,1,0:T(1,128)} %broadcast.445), channel_id=1, source_target_pairs={{1,0},{2,1},{3,2},{4,3},{5,4},{6,5},{7,6},{8,7},{9,8},{10,9},{11,1... | collective-permute-start | bytes 36872 | tf_op jit(solution)/shard_map/ppermute | solution.py:23
  129.3 151.6 %collective-permute-start = (f32[1,1,4096]{2,1,0:T(1,128)S(1)}, f32[1,1,4096]{2,1,0:T(1,128)S(1)}, u32[]{:S(2)}, u32[]{:S(2)}) collective-permute-start(f32[1,1,4096]{2,1,0:T(1,128)S(1)} %get-tuple-element.39), channel_id=1, source_target_pairs={{0,1},{1,2},{2,3},{3,4},{4,5},{5,6},{6,7},{7,8},{8,9},{9,10},{10,1... | collective-permute-start | bytes 49160 | tf_op jit(solution)/shard_map/ppermute | solution.py:21
  134.9 151.5 %collective-permute-start.1 = (f32[1,1,4096]{2,1,0:T(1,128)S(1)}, f32[1,1,4096]{2,1,0:T(1,128)S(1)}, u32[]{:S(2)}, u32[]{:S(2)}) collective-permute-start(f32[1,1,4096]{2,1,0:T(1,128)S(1)} %get-tuple-element.40), channel_id=1, source_target_pairs={{1,0},{2,1},{3,2},{4,3},{5,4},{6,5},{7,6},{8,7},{9,8},{10,9},{11,1... | collective-permute-start | bytes 49160 | tf_op jit(solution)/shard_map/ppermute | solution.py:23
  280.9 12.7 %collective-permute-start.2 = (f32[3,1,4096]{2,1,0:T(1,128)S(1)}, f32[3,1,4096]{2,1,0:T(1,128)S(1)}, u32[]{:S(2)}, u32[]{:S(2)}) collective-permute-start(f32[3,1,4096]{2,1,0:T(1,128)S(1)} %get-tuple-element.30), channel_id=1, source_target_pairs={{0,1},{1,2},{2,3},{3,4},{4,5},{5,6},{6,7},{7,8},{8,9},{9,10},{10,1... | collective-permute-start | bytes 147464 | tf_op jit(solution)/shard_map/ppermute | solution.py:21
  286.5 15.0 %collective-permute-start.3 = (f32[3,1,4096]{2,1,0:T(1,128)S(1)}, f32[3,1,4096]{2,1,0:T(1,128)S(1)}, u32[]{:S(2)}, u32[]{:S(2)}) collective-permute-start(f32[3,1,4096]{2,1,0:T(1,128)S(1)} %get-tuple-element.31), channel_id=1, source_target_pairs={{1,0},{2,1},{3,2},{4,3},{5,4},{6,5},{7,6},{8,7},{9,8},{10,9},{11,1... | collective-permute-start | bytes 147464 | tf_op jit(solution)/shard_map/ppermute | solution.py:23
  293.6 11.9 %collective-permute-start.8 = (f32[1,1,1024]{2,1,0:T(1,128)S(1)}, f32[1,1,1024]{2,1,0:T(1,128)S(1)}, u32[]{:S(2)}, u32[]{:S(2)}) collective-permute-start(f32[1,1,1024]{2,1,0:T(1,128)S(1)} %get-tuple-element.73), channel_id=1, source_target_pairs={{0,1},{1,2},{2,3},{3,4},{4,5},{5,6},{6,7},{7,8},{8,9},{9,10},{10,1... | collective-permute-start | bytes 12296 | tf_op jit(solution)/shard_map/ppermute | solution.py:21
  301.5 11.9 %collective-permute-start.9 = (f32[1,1,1024]{2,1,0:T(1,128)S(1)}, f32[1,1,1024]{2,1,0:T(1,128)S(1)}, u32[]{:S(2)}, u32[]{:S(2)}) collective-permute-start(f32[1,1,1024]{2,1,0:T(1,128)S(1)} %get-tuple-element.74), channel_id=1, source_target_pairs={{1,0},{2,1},{3,2},{4,3},{5,4},{6,5},{7,6},{8,7},{9,8},{10,9},{11,1... | collective-permute-start | bytes 12296 | tf_op jit(solution)/shard_map/ppermute | solution.py:23
  305.5 10.6 %collective-permute-start.4 = (f32[3,1,4096]{2,1,0:T(1,128)S(1)}, f32[3,1,4096]{2,1,0:T(1,128)S(1)}, u32[]{:S(2)}, u32[]{:S(2)}) collective-permute-start(f32[3,1,4096]{2,1,0:T(1,128)S(1)} %get-tuple-element.28), channel_id=1, source_target_pairs={{0,1},{1,2},{2,3},{3,4},{4,5},{5,6},{6,7},{7,8},{8,9},{9,10},{10,1... | collective-permute-start | bytes 147464 | tf_op jit(solution)/shard_map/ppermute | solution.py:21
  313.4 9.6 collective-permute-start.5
  325.1 6.1 collective-permute-start.6
  327.1 10.6 %collective-permute-start.7 = (f32[3,1,4096]{2,1,0:T(1,128)S(1)}, f32[3,1,4096]{2,1,0:T(1,128)S(1)}, u32[]{:S(2)}, u32[]{:S(2)}) collective-permute-start(f32[3,1,4096]{2,1,0:T(1,128)S(1)} %get-tuple-element.27), channel_id=1, source_target_pairs={{1,0},{2,1},{3,2},{4,3},{5,4},{6,5},{7,6},{8,7},{9,8},{10,9},{11,1... | collective-permute-start | bytes 147464 | tf_op jit(solution)/shard_map/ppermute | solution.py:23
  331.2 204.4 %collective-permute-start.10 = (f32[3,1,1024]{2,1,0:T(1,128)}, f32[3,1,1024]{2,1,0:T(1,128)}, u32[]{:S(2)}, u32[]{:S(2)}) collective-permute-start(f32[3,1,1024]{2,1,0:T(1,128)} %broadcast.445), channel_id=1, source_target_pairs={{0,1},{1,2},{2,3},{3,4},{4,5},{5,6},{6,7},{7,8},{8,9},{9,10},{10,1... | collective-permute-start | bytes 36872 | tf_op jit(solution)/shard_map/ppermute | solution.py:21
  337.7 205.8 %collective-permute-start.16 = (f32[1,1,256]{2,1,0:T(1,128)}, f32[1,1,256]{2,1,0:T(1,128)}, u32[]{:S(2)}, u32[]{:S(2)}) collective-permute-start(f32[1,1,256]{2,1,0:T(1,128)} %get-tuple-element.89), channel_id=1, source_target_pairs={{0,1},{1,2},{2,3},{3,4},{4,5},{5,6},{6,7},{7,8},{8,9},{9,10},{10,1... | collective-permute-start | bytes 3080 | tf_op jit(solution)/shard_map/ppermute | solution.py:21
  532.2 13.2 %collective-permute-start.17 = (f32[1,1,256]{2,1,0:T(1,128)}, f32[1,1,256]{2,1,0:T(1,128)S(1)}, u32[]{:S(2)}, u32[]{:S(2)}) collective-permute-start(f32[1,1,256]{2,1,0:T(1,128)} %get-tuple-element.90), channel_id=1, source_target_pairs={{1,0},{2,1},{3,2},{4,3},{5,4},{6,5},{7,6},{8,7},{9,8},{10,9},{11,1... | collective-permute-start | bytes 3080 | tf_op jit(solution)/shard_map/ppermute | solution.py:23
  537.1 9.8 collective-permute-start.12
  543.5 9.2 collective-permute-start.13
  554.0 7.0 collective-permute-start.14
  556.0 9.2 collective-permute-start.15
  591.4 13.6 %collective-permute-start.20 = (f32[3,1,256]{2,1,0:T(1,128)S(1)}, f32[3,1,256]{2,1,0:T(1,128)S(1)}, u32[]{:S(2)}, u32[]{:S(2)}) collective-permute-start(f32[3,1,256]{2,1,0:T(1,128)S(1)} %get-tuple-element.81), channel_id=1, source_target_pairs={{0,1},{1,2},{2,3},{3,4},{4,5},{5,6},{6,7},{7,8},{8,9},{9,10},{10,1... | collective-permute-start | bytes 9224 | tf_op jit(solution)/shard_map/ppermute | solution.py:21
  593.7 11.4 %collective-permute-start.21 = (f32[3,1,256]{2,1,0:T(1,128)S(1)}, f32[3,1,256]{2,1,0:T(1,128)S(1)}, u32[]{:S(2)}, u32[]{:S(2)}) collective-permute-start(f32[3,1,256]{2,1,0:T(1,128)S(1)} %get-tuple-element.82), channel_id=1, source_target_pairs={{1,0},{2,1},{3,2},{4,3},{5,4},{6,5},{7,6},{8,7},{9,8},{10,9},{11,1... | collective-permute-start | bytes 9224 | tf_op jit(solution)/shard_map/ppermute | solution.py:23
  597.3 55.3 %collective-permute-start.27 = (f32[3,1,64]{2,0,1:T(4,128)}, f32[3,1,64]{2,0,1:T(4,128)}, u32[]{:S(2)}, u32[]{:S(2)}) collective-permute-start(f32[3,1,64]{2,0,1:T(4,128)} %broadcast.453), channel_id=1, source_target_pairs={{16,0},{32,16},{48,32},{64,48},{80,64},{96,80},{112,96},{17,1},{33... | collective-permute-start | bytes 2312 | tf_op jit(solution)/shard_map/ppermute | solution.py:23
  599.2 53.4 %collective-permute-start.26 = (f32[3,1,64]{2,0,1:T(4,128)}, f32[3,1,64]{2,0,1:T(4,128)}, u32[]{:S(2)}, u32[]{:S(2)}) collective-permute-start(f32[3,1,64]{2,0,1:T(4,128)} %broadcast.453), channel_id=1, source_target_pairs={{0,16},{16,32},{32,48},{48,64},{64,80},{80,96},{96,112},{1,17},{17... | collective-permute-start | bytes 2312 | tf_op jit(solution)/shard_map/ppermute | solution.py:21
  605.2 7.9 collective-permute-start.22
  610.7 9.1 collective-permute-start.23
  639.8 9.6 collective-permute-start.24
  655.7 4.9 collective-permute-start.29
  663.0 4.9 collective-permute-start.31
  670.2 4.9 collective-permute-start.33
  677.4 4.9 collective-permute-start.35
  684.7 4.9 collective-permute-start.37
  693.2 5.1 collective-permute-start.39
  702.1 4.9 collective-permute-start.41
  711.9 6.0 collective-permute-start.42
  716.0 9.1 collective-permute-start.43
  725.3 5.3 collective-permute-start.44
  727.3 9.1 collective-permute-start.45
  754.6 5.3 collective-permute-start.46
  756.5 9.2 collective-permute-start.47
  767.0 5.5 collective-permute-start.48
  769.0 9.2 collective-permute-start.49
  954.5 5.3 collective-permute-start.50
  956.4 9.6 collective-permute-start.51
  968.2 5.5 collective-permute-start.52
  970.2 9.6 collective-permute-start.53
  (73 other events, 4104.1 us)
Sparse Core Ops, SparseCore 0:
  9.5 70.7 all-gather.4
  82.5 154.1 all-gather.2
where the time goes:
time: 1020 us; the launch traced here: 1010 us
  local copies, waits for them, and re-layouts  462 us (45%)
  waiting for transfers between devices  236 us (23%)
  starting transfers between devices  169 us (17%)
  other arithmetic  115 us (11%)
  between operations  15.6 us (2%)
  blocking collectives  15.4 us (2%)
    reshape x3, local copies, waits for them, and re-layouts, coarsen(): grid.reshape(channels, length // 2, 2, width_y // 2, 2, width_y // 2, 2)  171 us
    reshape x3, local copies, waits for them, and re-layouts, refine(): return shaped.reshape(channels, 2 * length, 4 * plane)  151 us
    ppermute x27, starting transfers between devices, padded_2(): lax.ppermute(tail, axis, [(i, (i + 1) % count) for i in range(ends)])  99.5 us
    all_gather x1, waiting for transfers between devices, local(): lax.all_gather(velocity_old, 'dev', axis=0, tiled=True)  96.1 us
    ppermute x27, waiting for transfers between devices, padded_2(): lax.ppermute(head, axis, [((i + 1) % count, i) for i in range(ends)])  80.7 us
    ppermute x27, starting transfers between devices, padded_2(): lax.ppermute(head, axis, [((i + 1) % count, i) for i in range(ends)])  69.5 us
    all_gather x1, waiting for transfers between devices, local(): lax.all_gather(viscosity_old, 'dev', axis=0, tiled=True)  57.7 us
    reduce_sum x6, other arithmetic, coarsen(): shaped.mean(axis=(2, 4, 6)).reshape(channels, length // 2, plane // 4)  55.9 us
  transfers between devices with their start and end apart: 56, of which 20 were waited for; matrix products, arithmetic and copies ran while one was open for 34% of the time, Pallas kernels for 0%

commit v1 on v0

--- a/solution.py
+++ b/solution.py
@@ -170,7 +170,9 @@
     wanted = mine_dev * blk_per + mine_slot
     pieces = (
         lax.all_gather(velocity_old, "dev", axis=0, tiled=True),
-        lax.all_gather(viscosity_old, "dev", axis=0, tiled=True),
+        jnp.concatenate(
+            lax.all_to_all(jnp.stack([viscosity_old] * lax.axis_size("dev")), "dev", 0, 0), axis=0
+        ),
     )
     piece_rows = pieces[0].shape[0]
     inside = (wanted >= 0) & (wanted < piece_rows)

time: 1020 us -> 1060 us (1.039)
  starting transfers between devices: 169 us -> 224 us
  waiting for transfers between devices: 236 us -> 208 us
  local copies, waits for them, and re-layouts: 462 us -> 478 us
    all_to_all x0 -> x1, waiting for transfers between devices: none -> 112 us  [local(): lax.all_to_all(jnp.stack([viscosity_old] * lax.axis_size('dev')), 'dev',...]
    all_gather x1, waiting for transfers between devices: 96.1 us -> 10.5 us  [local(): lax.all_gather(velocity_old, 'dev', axis=0, tiled=True)]
    all_gather x1 -> x0, waiting for transfers between devices: 57.7 us -> none  [local(): lax.all_gather(viscosity_old, 'dev', axis=0, tiled=True)]
    ppermute x27, starting transfers between devices: 99.5 us -> 148 us  [padded_2(): lax.ppermute(tail, axis, [(i, (i + 1) % count) for i in range(ends)])]
  transfers between devices with their start and end apart: 56 -> 56, of which waited for: 20 -> 21; matrix products, arithmetic and copies ran while one was open for 34% -> 34% of each run, Pallas kernels for 0% -> 0%
where the time goes in v1:
time: 1060 us; the launch traced here: 1050 us
  local copies, waits for them, and re-layouts  478 us (45%)
  starting transfers between devices  224 us (21%)
  waiting for transfers between devices  208 us (20%)
  other arithmetic  113 us (11%)
  between operations  15.6 us (1%)
  blocking collectives  15.4 us (1%)
    reshape x3, local copies, waits for them, and re-layouts, coarsen(): grid.reshape(channels, length // 2, 2, width_y // 2, 2, width_y // 2, 2)  171 us
    reshape x3, local copies, waits for them, and re-layouts, refine(): return shaped.reshape(channels, 2 * length, 4 * plane)  151 us
    ppermute x27, starting transfers between devices, padded_2(): lax.ppermute(tail, axis, [(i, (i + 1) % count) for i in range(ends)])  148 us
    all_to_all x1, waiting for transfers between devices, local(): lax.all_to_all(jnp.stack([viscosity_old] * lax.axis_size('dev')), 'dev',...  112 us
    ppermute x27, waiting for transfers between devices, padded_2(): lax.ppermute(head, axis, [((i + 1) % count, i) for i in range(ends)])  84.6 us
    ppermute x27, starting transfers between devices, padded_2(): lax.ppermute(head, axis, [((i + 1) % count, i) for i in range(ends)])  68.8 us
    reduce_sum x6, other arithmetic, coarsen(): shaped.mean(axis=(2, 4, 6)).reshape(channels, length // 2, plane // 4)  55.8 us
    broadcast_in_dim x6, local copies, waits for them, and re-layouts, refine(): jnp.broadcast_to(shaped, (channels, length, 2, width_y, 2, width_y, 2))  42.3 us
  transfers between devices with their start and end apart: 56, of which 21 were waited for; matrix products, arithmetic and copies ran while one was open for 34% of the time, Pallas kernels for 0%

profile of v1, /device:TPU:31, one launch (start us, length us, event | category | flops | bytes accessed | tf_op | source)
XLA Modules:
  0.0 1053.7 jit_solution(6212185109947118065)
XLA Ops:
  7.6 4.4 stack.2
  12.0 6.5 all-to-all-start
  19.1 4.2 collective-permute-start.10
  25.9 7.8 collective-permute-start.18
  35.5 111.6 %all-to-all-done = f32[16,4,32,1024]{3,2,1,0:T(8,128)} async-done(((f32[16,4,32,1024]{3,2,1,0:T(8,128)}), f32[16,4,32,1024]{3,2,1,0:T(8,128)}, u32[]{:S(2)}, u32[]{:S(2)}) %all-to-all-start) | async-done | bytes 8388640 | tf_op jit(solution)/shard_map/all_to_all | solution.py:174
  147.1 4.0 gather_fusion.1
  157.9 4.6 copy.71
  162.5 22.2 %reshape_reshape.2 = f32[16,2,32,2,32,2]{1,0,5,4,3,2:T(8,128)} reshape(f32[1,1,32,2,32,2,32]{2,6,5,4,3,1,0:T(8,128)} %copy.72) | data formatting | bytes 1048576 | tf_op jit(solution)/shard_map/reshape;reshape | solution.py:98
  184.7 12.6 %reduce_sum.55 = f32[16,32,32]{0,2,1:T(8,128)S(1)} reduce(f32[16,2,32,2,32,2]{1,0,5,4,3,2:T(8,128)} %reshape_reshape.2, f32[]{:T(128)} %constant.250.clone.1), dimensions={1,3,5}, to_apply=%region_1.2 | reduce | flops 114688 | bytes 589828 | tf_op jit(solution)/shard_map/reduce_sum | solution.py:99
  201.4 4.3 reshape.255
  205.8 45.1 %collective-permute-start = (f32[1,1,4096]{2,1,0:T(1,128)S(1)}, f32[1,1,4096]{2,1,0:T(1,128)S(1)}, u32[]{:S(2)}, u32[]{:S(2)}) collective-permute-start(f32[1,1,4096]{2,1,0:T(1,128)S(1)} %get-tuple-element.39), channel_id=1, source_target_pairs={{0,1},{1,2},{2,3},{3,4},{4,5},{5,6},{6,7},{7,8},{8,9},{9,10},{10,1... | collective-permute-start | bytes 49160 | tf_op jit(solution)/shard_map/ppermute | solution.py:21
  256.3 10.5 all-gather.2.cloned.1.call-done
  266.8 8.8 gather_fusion
  275.6 4.1 gather.13
  279.7 10.0 copy.70
  289.7 11.8 %select_bitcast_fusion = f32[3,1,32,2,32,2,32]{6,5,4,3,2,0,1:T(2,128)} fusion(f32[1,2,2,3,32,32,32]{5,2,4,1,6,3,0:T(2,128)} %copy.70, pred[2,2]{1,0:T(4,128)(4,1)S(1)} %compare_and_fusion, pred[2,2]{1,0:T(4,128)(4,1)S(1)} %and.182), kind=kLoop, calls=%fused_computation.2 | loop fusion | flops 786432 | bytes 3145736 | tf_op jit(solution)/shard_map/transpose | solution.py:34
  301.5 9.5 reshape.253
  311.1 13.6 %collective-permute-start.2 = (f32[3,1,4096]{2,1,0:T(1,128)S(1)}, f32[3,1,4096]{2,1,0:T(1,128)S(1)}, u32[]{:S(2)}, u32[]{:S(2)}) collective-permute-start(f32[3,1,4096]{2,1,0:T(1,128)S(1)} %get-tuple-element.30), channel_id=1, source_target_pairs={{0,1},{1,2},{2,3},{3,4},{4,5},{5,6},{6,7},{7,8},{8,9},{9,10},{10,1... | collective-permute-start | bytes 147464 | tf_op jit(solution)/shard_map/ppermute | solution.py:21
  326.7 5.2 add_bitcast_fusion
  331.9 7.9 collective-permute-start.8
  343.8 7.9 collective-permute-start.4
  354.4 6.9 collective-permute-done.5
  375.0 4.5 collective-permute-start.16
  382.6 154.0 %reshape.256 = f32[3,16,2,32,2,32,2]{6,5,4,3,2,1,0:T(8,128)} reshape(f32[3,32,4096]{2,1,0:T(8,128)} %fusion.34) | data formatting | bytes 3145728 | tf_op jit(solution)/shard_map/reshape | solution.py:98
  536.6 31.6 %reduce_sum.54 = f32[3,16,32,32]{3,2,1,0:T(8,128)} reduce(f32[3,16,2,32,2,32,2]{6,5,4,3,2,1,0:T(8,128)} %reshape.256, f32[]{:T(128)} %constant.250.clone.1), dimensions={2,4,6}, to_apply=%region_0.1 | reduce | flops 344064 | bytes 1769476 | tf_op jit(solution)/shard_map/reduce_sum | solution.py:99
  575.3 7.9 collective-permute-start.12
  586.6 5.9 collective-permute-done.13
  600.7 4.3 collective-permute-done.15
  606.6 14.7 %reshape.257 = f32[3,8,2,16,2,16,2]{6,5,4,3,2,1,0:T(8,128)} reshape(f32[3,16,1024]{2,1,0:T(8,128)} %fusion.105) | data formatting | bytes 393216 | tf_op jit(solution)/shard_map/reshape | solution.py:98
  621.3 6.3 reduce_sum.56
  644.3 7.4 collective-permute-start.22
  654.1 6.7 collective-permute-done.23
  665.4 15.4 %all_gather.7 = f32[4,64,64]{2,0,1:T(4,128)S(1)} all-gather(f32[4,4,64]{2,0,1:T(4,128)S(1)} %copy.75), channel_id=1, replica_groups=mesh['grp'=8,'dev'=16] {'dev'}, dimensions={1}, use_global_device_ids=true | all-gather | bytes 69632 | tf_op jit(solution)/shard_map/all_gather | solution.py:120
  680.8 6.6 collective-permute-start.24
  752.3 4.1 collective-permute-start.42
  758.3 7.2 collective-permute-done.43
  771.0 5.8 collective-permute-done.45
  777.7 5.7 broadcast_in_dim.360
  783.5 10.4 reshape.260
  800.2 5.9 collective-permute-done.47
  812.9 5.7 collective-permute-done.49
  821.7 32.2 %broadcast_in_dim.362 = f32[3,16,2,32,2,32,2]{6,5,4,3,2,1,0:T(8,128)} broadcast(f32[3,16,32,32]{3,2,1,0:T(8,128)} %broadcast_in_dim.361), dimensions={0,1,3,5} | broadcast | bytes 1769472 | tf_op jit(solution)/shard_map/broadcast_in_dim | solution.py:106
  853.9 138.6 %reshape.261 = f32[3,32,4096]{2,1,0:T(8,128)} reshape(f32[3,16,2,32,2,32,2]{6,5,4,3,2,1,0:T(8,128)} %broadcast_in_dim.362) | data formatting | bytes 3145728 | tf_op jit(solution)/shard_map/reshape | solution.py:107
  1000.1 6.3 collective-permute-done.51
  1014.1 6.0 collective-permute-done.53
  1023.0 7.7 reshape.262
  1030.7 10.0 copy.77
  1040.8 5.9 reshape.263
  (332 shorter events, 197.8 us)
Async XLA Ops:
  6.5 260.3 %all-gather.2.cloned.1.call-start = ((), (), s32[]{:S(2)}) async-start(), calls=%async_computation.1 | async-start | bytes 26738688 | tf_op jit(solution)/shard_map/all_gather | solution.py:172
  12.0 135.1 %all-to-all-start = ((f32[16,4,32,1024]{3,2,1,0:T(8,128)}), f32[16,4,32,1024]{3,2,1,0:T(8,128)}, u32[]{:S(2)}, u32[]{:S(2)}) async-start(f32[16,4,32,1024]{3,2,1,0:T(8,128)} %stack.2), calls=%async_computation | async-start | bytes 16777216 | tf_op jit(solution)/shard_map/all_to_all | solution.py:174
  19.1 552.8 %collective-permute-start.10 = (f32[3,1,1024]{2,1,0:T(1,128)}, f32[3,1,1024]{2,1,0:T(1,128)}, u32[]{:S(2)}, u32[]{:S(2)}) collective-permute-start(f32[3,1,1024]{2,1,0:T(1,128)} %broadcast.447), channel_id=1, source_target_pairs={{0,1},{1,2},{2,3},{3,4},{4,5},{5,6},{6,7},{7,8},{8,9},{9,10},{10,1... | collective-permute-start | bytes 36872 | tf_op jit(solution)/shard_map/ppermute | solution.py:21
  23.3 550.6 %collective-permute-start.11 = (f32[3,1,1024]{2,1,0:T(1,128)}, f32[3,1,1024]{2,1,0:T(1,128)}, u32[]{:S(2)}, u32[]{:S(2)}) collective-permute-start(f32[3,1,1024]{2,1,0:T(1,128)} %broadcast.447), channel_id=1, source_target_pairs={{1,0},{2,1},{3,2},{4,3},{5,4},{6,5},{7,6},{8,7},{9,8},{10,9},{11,1... | collective-permute-start | bytes 36872 | tf_op jit(solution)/shard_map/ppermute | solution.py:23
  25.9 604.4 %collective-permute-start.18 = (f32[3,1,256]{2,1,0:T(1,128)}, f32[3,1,256]{2,1,0:T(1,128)}, u32[]{:S(2)}, u32[]{:S(2)}) collective-permute-start(f32[3,1,256]{2,1,0:T(1,128)} %broadcast.451), channel_id=1, source_target_pairs={{0,1},{1,2},{2,3},{3,4},{4,5},{5,6},{6,7},{7,8},{8,9},{9,10},{10,1... | collective-permute-start | bytes 9224 | tf_op jit(solution)/shard_map/ppermute | solution.py:21
  205.8 105.3 %collective-permute-start = (f32[1,1,4096]{2,1,0:T(1,128)S(1)}, f32[1,1,4096]{2,1,0:T(1,128)S(1)}, u32[]{:S(2)}, u32[]{:S(2)}) collective-permute-start(f32[1,1,4096]{2,1,0:T(1,128)S(1)} %get-tuple-element.39), channel_id=1, source_target_pairs={{0,1},{1,2},{2,3},{3,4},{4,5},{5,6},{6,7},{7,8},{8,9},{9,10},{10,1... | collective-permute-start | bytes 49160 | tf_op jit(solution)/shard_map/ppermute | solution.py:21
  250.9 73.8 %collective-permute-start.1 = (f32[1,1,4096]{2,1,0:T(1,128)S(1)}, f32[1,1,4096]{2,1,0:T(1,128)S(1)}, u32[]{:S(2)}, u32[]{:S(2)}) collective-permute-start(f32[1,1,4096]{2,1,0:T(1,128)S(1)} %get-tuple-element.40), channel_id=1, source_target_pairs={{1,0},{2,1},{3,2},{4,3},{5,4},{6,5},{7,6},{8,7},{9,8},{10,9},{11,1... | collective-permute-start | bytes 49160 | tf_op jit(solution)/shard_map/ppermute | solution.py:23
  311.1 20.8 %collective-permute-start.2 = (f32[3,1,4096]{2,1,0:T(1,128)S(1)}, f32[3,1,4096]{2,1,0:T(1,128)S(1)}, u32[]{:S(2)}, u32[]{:S(2)}) collective-permute-start(f32[3,1,4096]{2,1,0:T(1,128)S(1)} %get-tuple-element.30), channel_id=1, source_target_pairs={{0,1},{1,2},{2,3},{3,4},{4,5},{5,6},{6,7},{7,8},{8,9},{9,10},{10,1... | collective-permute-start | bytes 147464 | tf_op jit(solution)/shard_map/ppermute | solution.py:21
  324.7 15.0 %collective-permute-start.3 = (f32[3,1,4096]{2,1,0:T(1,128)S(1)}, f32[3,1,4096]{2,1,0:T(1,128)S(1)}, u32[]{:S(2)}, u32[]{:S(2)}) collective-permute-start(f32[3,1,4096]{2,1,0:T(1,128)S(1)} %get-tuple-element.31), channel_id=1, source_target_pairs={{1,0},{2,1},{3,2},{4,3},{5,4},{6,5},{7,6},{8,7},{9,8},{10,9},{11,1... | collective-permute-start | bytes 147464 | tf_op jit(solution)/shard_map/ppermute | solution.py:23
  331.9 11.9 %collective-permute-start.8 = (f32[1,1,1024]{2,1,0:T(1,128)S(1)}, f32[1,1,1024]{2,1,0:T(1,128)S(1)}, u32[]{:S(2)}, u32[]{:S(2)}) collective-permute-start(f32[1,1,1024]{2,1,0:T(1,128)S(1)} %get-tuple-element.73), channel_id=1, source_target_pairs={{0,1},{1,2},{2,3},{3,4},{4,5},{5,6},{6,7},{7,8},{8,9},{9,10},{10,1... | collective-permute-start | bytes 12296 | tf_op jit(solution)/shard_map/ppermute | solution.py:21
  339.8 11.9 %collective-permute-start.9 = (f32[1,1,1024]{2,1,0:T(1,128)S(1)}, f32[1,1,1024]{2,1,0:T(1,128)S(1)}, u32[]{:S(2)}, u32[]{:S(2)}) collective-permute-start(f32[1,1,1024]{2,1,0:T(1,128)S(1)} %get-tuple-element.74), channel_id=1, source_target_pairs={{1,0},{2,1},{3,2},{4,3},{5,4},{6,5},{7,6},{8,7},{9,8},{10,9},{11,1... | collective-permute-start | bytes 12296 | tf_op jit(solution)/shard_map/ppermute | solution.py:23
  343.8 10.6 %collective-permute-start.4 = (f32[3,1,4096]{2,1,0:T(1,128)S(1)}, f32[3,1,4096]{2,1,0:T(1,128)S(1)}, u32[]{:S(2)}, u32[]{:S(2)}) collective-permute-start(f32[3,1,4096]{2,1,0:T(1,128)S(1)} %get-tuple-element.28), channel_id=1, source_target_pairs={{0,1},{1,2},{2,3},{3,4},{4,5},{5,6},{6,7},{7,8},{8,9},{9,10},{10,1... | collective-permute-start | bytes 147464 | tf_op jit(solution)/shard_map/ppermute | solution.py:21
  351.7 9.6 collective-permute-start.5
  363.4 6.1 collective-permute-start.6
  365.4 9.6 collective-permute-start.7
  369.5 260.8 %collective-permute-start.19 = (f32[3,1,256]{2,1,0:T(1,128)}, f32[3,1,256]{2,1,0:T(1,128)}, u32[]{:S(2)}, u32[]{:S(2)}) collective-permute-start(f32[3,1,256]{2,1,0:T(1,128)} %broadcast.451), channel_id=1, source_target_pairs={{1,0},{2,1},{3,2},{4,3},{5,4},{6,5},{7,6},{8,7},{9,8},{10,9},{11,1... | collective-permute-start | bytes 9224 | tf_op jit(solution)/shard_map/ppermute | solution.py:23
  375.0 208.2 %collective-permute-start.16 = (f32[1,1,256]{2,1,0:T(1,128)}, f32[1,1,256]{2,1,0:T(1,128)}, u32[]{:S(2)}, u32[]{:S(2)}) collective-permute-start(f32[1,1,256]{2,1,0:T(1,128)} %get-tuple-element.89), channel_id=1, source_target_pairs={{0,1},{1,2},{2,3},{3,4},{4,5},{5,6},{6,7},{7,8},{8,9},{9,10},{10,1... | collective-permute-start | bytes 3080 | tf_op jit(solution)/shard_map/ppermute | solution.py:21
  571.9 13.2 %collective-permute-start.17 = (f32[1,1,256]{2,1,0:T(1,128)}, f32[1,1,256]{2,1,0:T(1,128)S(1)}, u32[]{:S(2)}, u32[]{:S(2)}) collective-permute-start(f32[1,1,256]{2,1,0:T(1,128)} %get-tuple-element.90), channel_id=1, source_target_pairs={{1,0},{2,1},{3,2},{4,3},{5,4},{6,5},{7,6},{8,7},{9,8},{10,9},{11,1... | collective-permute-start | bytes 3080 | tf_op jit(solution)/shard_map/ppermute | solution.py:23
  575.3 11.2 %collective-permute-start.12 = (f32[3,1,1024]{2,1,0:T(1,128)S(1)}, f32[3,1,1024]{2,1,0:T(1,128)S(1)}, u32[]{:S(2)}, u32[]{:S(2)}) collective-permute-start(f32[3,1,1024]{2,1,0:T(1,128)S(1)} %get-tuple-element.47), channel_id=1, source_target_pairs={{0,1},{1,2},{2,3},{3,4},{4,5},{5,6},{6,7},{7,8},{8,9},{9,10},{10,1... | collective-permute-start | bytes 36872 | tf_op jit(solution)/shard_map/ppermute | solution.py:21
  583.2 9.2 collective-permute-start.13
  593.7 7.0 collective-permute-start.14
  595.7 9.2 collective-permute-start.15
  631.2 12.9 %collective-permute-start.20 = (f32[3,1,256]{2,1,0:T(1,128)S(1)}, f32[3,1,256]{2,1,0:T(1,128)S(1)}, u32[]{:S(2)}, u32[]{:S(2)}) collective-permute-start(f32[3,1,256]{2,1,0:T(1,128)S(1)} %get-tuple-element.81), channel_id=1, source_target_pairs={{0,1},{1,2},{2,3},{3,4},{4,5},{5,6},{6,7},{7,8},{8,9},{9,10},{10,1... | collective-permute-start | bytes 9224 | tf_op jit(solution)/shard_map/ppermute | solution.py:21
  633.4 10.7 %collective-permute-start.21 = (f32[3,1,256]{2,1,0:T(1,128)S(1)}, f32[3,1,256]{2,1,0:T(1,128)S(1)}, u32[]{:S(2)}, u32[]{:S(2)}) collective-permute-start(f32[3,1,256]{2,1,0:T(1,128)S(1)} %get-tuple-element.82), channel_id=1, source_target_pairs={{1,0},{2,1},{3,2},{4,3},{5,4},{6,5},{7,6},{8,7},{9,8},{10,9},{11,1... | collective-permute-start | bytes 9224 | tf_op jit(solution)/shard_map/ppermute | solution.py:23
  637.1 55.6 %collective-permute-start.26 = (f32[3,1,64]{2,0,1:T(4,128)}, f32[3,1,64]{2,0,1:T(4,128)}, u32[]{:S(2)}, u32[]{:S(2)}) collective-permute-start(f32[3,1,64]{2,0,1:T(4,128)} %broadcast.455), channel_id=1, source_target_pairs={{0,16},{16,32},{32,48},{48,64},{64,80},{80,96},{96,112},{1,17},{17... | collective-permute-start | bytes 2312 | tf_op jit(solution)/shard_map/ppermute | solution.py:21
  639.0 53.7 %collective-permute-start.27 = (f32[3,1,64]{2,0,1:T(4,128)}, f32[3,1,64]{2,0,1:T(4,128)}, u32[]{:S(2)}, u32[]{:S(2)}) collective-permute-start(f32[3,1,64]{2,0,1:T(4,128)} %broadcast.455), channel_id=1, source_target_pairs={{16,0},{32,16},{48,32},{64,48},{80,64},{96,80},{112,96},{17,1},{33... | collective-permute-start | bytes 2312 | tf_op jit(solution)/shard_map/ppermute | solution.py:23
  644.3 9.9 collective-permute-start.22
  651.7 9.1 collective-permute-start.23
  680.8 8.6 collective-permute-start.24
  695.8 5.1 collective-permute-start.29
  703.2 4.9 collective-permute-start.31
  710.5 4.9 collective-permute-start.33
  717.7 4.9 collective-permute-start.35
  731.5 4.9 collective-permute-start.38
  733.4 5.2 collective-permute-start.39
  742.4 4.9 collective-permute-start.41
  752.3 6.0 collective-permute-start.42
  756.4 9.1 collective-permute-start.43
  765.7 5.3 collective-permute-start.44
  767.7 9.1 collective-permute-start.45
  794.9 5.3 collective-permute-start.46
  796.9 9.2 collective-permute-start.47
  807.4 5.5 collective-permute-start.48
  809.4 9.2 collective-permute-start.49
  994.8 5.3 collective-permute-start.50
  996.7 9.6 collective-permute-start.51
  1008.5 5.5 collective-permute-start.52
  1010.5 9.6 collective-permute-start.53
  (75 other events, 4189.8 us)
Sparse Core Ops, SparseCore 0:
  9.6 257.2 all-gather.1
